TPU v7x, 256 devices: a whole 4x4x8 slice. The times are simulated.
256 devices in a mesh: rows: 64 (over y, z, core), groups: 4 (over x).
Axes of the slice: x: 4, y: 4, z: 8, core: 2. Of those that a mesh axis runs over, the one named last changes fastest.
Arguments:
- snapshots: bfloat16 [131072, 1024], P('rows', 'groups'), may hold values from -6 to 6
- mass_diag: float32 [131072], P('rows'), may hold values from 0.5 to 2
- lower_coupling: float32 [64, 128, 128], P('rows'), may hold values from -0.5 to 0.5
- upper_coupling: float32 [64, 128, 128], P('rows'), may hold values from -0.5 to 0.5
- band_offsets: int32 [64, 2], P('rows'), may hold values from 1 to 2
- start_basis: float32 [1024, 512], replicated, may hold values from -6 to 6
Outputs:
- modes: float32 [131072, 512], P('rows', 'groups')
All inputs are finite; a program needn't handle non-finite values.
Results may differ from a plain program's by a relative error of at most 0.0042.
Values may be sent and summed in bfloat16 or wider, within the bound.
No kernel may reach another device: no remote copies, remote signals or barrier semaphores. Data moves between devices by JAX's collectives and lax.ppermute only.
A program may use at most 128 MiB of HBM per device.

v0:
```python
import jax
import jax.numpy as jnp
from jax import lax
from jax.sharding import PartitionSpec as P

ITERS = 3


def from_behind(value, axis, by):
    devices = lax.axis_size(axis)
    pairs = [(i, i + by) for i in range(devices) if 0 <= i + by < devices]
    return lax.ppermute(value, axis, pairs)


def orthonormal(image):
    correlation = jnp.dot(
        image.T, image, precision=lax.Precision.HIGHEST, preferred_element_type=jnp.float32
    )
    lower = jnp.linalg.cholesky(correlation)
    return lax.linalg.triangular_solve(lower, image, left_side=False, lower=True, transpose_a=True)


def pass_down(piece):
    return from_behind(piece, "rows", 1)


def pass_up(piece):
    return from_behind(piece, "rows", -1)


def shards(snapshots, mass_diag, lower_coupling, upper_coupling, band_offsets, start_basis):
    block_rows = snapshots.shape[0]
    rim_rows = lower_coupling.shape[1]
    total_rows = block_rows * lax.axis_size("rows")
    bottom_rim = snapshots[block_rows - rim_rows :, :]
    top_rim = snapshots[:rim_rows, :]
    below_one = pass_down(bottom_rim)
    below_two = pass_down(below_one)
    above_one = pass_up(top_rim)
    above_two = pass_up(above_one)
    lower_rims = jnp.where(band_offsets[0, 0] == 1, below_one, below_two).astype(jnp.float32)
    upper_rims = jnp.where(band_offsets[0, 1] == 1, above_one, above_two).astype(jnp.float32)
    lower_terms = jnp.dot(
        lower_coupling[0],
        lower_rims,
        precision=lax.Precision.HIGHEST,
        preferred_element_type=jnp.float32,
    )
    upper_terms = jnp.dot(
        upper_coupling[0],
        upper_rims,
        precision=lax.Precision.HIGHEST,
        preferred_element_type=jnp.float32,
    )
    weighted = mass_diag[:, None] * snapshots.astype(jnp.float32)
    weighted = weighted.at[:rim_rows, :].add(lower_terms)
    weighted = weighted.at[block_rows - rim_rows :, :].add(upper_terms)
    weighted = weighted.astype(jnp.bfloat16)
    gathered = lax.all_gather(weighted, "groups", axis=1, tiled=True)
    gram_cols = lax.dot_general(
        gathered, weighted, (((0,), (0,)), ((), ())), preferred_element_type=jnp.float32
    )
    gram_cols = lax.psum(gram_cols, "rows") / total_rows
    basis = start_basis
    gram = lax.all_gather(gram_cols, "groups", axis=1, tiled=True)
    for turn_index in range(ITERS):
        image = jnp.dot(
            gram, basis, precision=lax.Precision.HIGHEST, preferred_element_type=jnp.float32
        )
        basis = orthonormal(image)
    basis_low = basis.astype(jnp.bfloat16)
    group_index = lax.axis_index("groups")
    mode_cols = basis_low.shape[1] // lax.axis_size("groups")
    basis_part = lax.dynamic_slice_in_dim(basis_low, group_index * mode_cols, mode_cols, 1)
    return jnp.dot(gathered, basis_part, preferred_element_type=jnp.float32)


def solution(mesh):
    placed = (
        P("rows", "groups"),
        P("rows"),
        P("rows", None, None),
        P("rows", None, None),
        P("rows", None),
        P(),
    )
    return jax.shard_map(
        shards, mesh=mesh, in_specs=placed, out_specs=P("rows", "groups"), check_vma=False
    )
```

profile of v0, /device:TPU:1, one launch (start us, length us, event | category | flops | bytes accessed | tf_op | source)
XLA Modules:
  0.0 840.2 jit_solution(3285702650154615542)
XLA Ops:
  7.6 4.9 collective-permute-start
  12.5 1.9 collective-permute-start.2
  16.3 3.6 collective-permute-start.1
  24.0 3.3 collective-permute-done.3
  28.8 54.4 %all-gather.3.cloned.1.call-done = bf16[2048,1024]{0,1:T(8,128)(2,1)} async-done(((bf16[2048,256]{0,1:T(8,128)(2,1)}), bf16[2048,1024]{0,1:T(8,128)(2,1)}) %all-gather.3.cloned.1.call-update) | async-done | bytes 4194320 | tf_op jit(solution)/shard_map/all_gather | solution.py:59
  83.2 4.8 fusion.159
  88.1 184.5 %all-reduce.3.cloned.1.call-done = f32[1024,256]{1,0:T(8,128)} async-done(((f32[1024,256]{1,0:T(8,128)}), f32[1024,256]{1,0:T(8,128)}) %all-reduce.3.cloned.1.call-update) | async-done | bytes 1048592 | tf_op jit(solution)/shard_map/psum | solution.py:63
  272.6 2.3 broadcast_multiply_fusion
  274.9 50.0 %all-gather.5.cloned.1.call-done = f32[1024,1024]{1,0:T(8,128)} async-done(((f32[1024,256]{1,0:T(8,128)}), f32[1024,1024]{1,0:T(8,128)}) %all-gather.5.cloned.1.call-update) | async-done | bytes 4194320 | tf_op jit(solution)/shard_map/all_gather | solution.py:65
  324.9 8.8 %fusion.160 = f32[1024,512]{1,0:T(8,128)S(1)} fusion(f32[1024,1024]{1,0:T(8,128)} %all-gather.5.cloned.1.call-done, f32[1024,512]{1,0:T(8,128)S(1)} %copy-done), kind=kOutput, calls=%fused_computation.247 | convolution fusion | flops 6442450944 | bytes 8388608 | tf_op jit(solution)/shard_map/dot_general | solution.py:67
  335.2 3.7 fusion.161
  342.6 11.7 %cholesky.374 = f32[128,128]{1,0:T(8,128)S(1)} custom-call(f32[128,128]{1,0:T(8,128)S(1)} %cholesky.586), custom_call_target="Cholesky" | custom-call | tf_op jit(solution)/shard_map/jit(cholesky)/cholesky | solution.py:19
  354.3 9.8 %custom-call.31 = f32[1,128,128]{1,2,0:T(8,128)S(1)} custom-call(f32[1,128,128]{2,1,0:T(8,128)S(1)} %get-tuple-element.115), custom_call_target="InvertDiagBlocksLowerTriangular" | custom-call | tf_op jit(solution)/shard_map/jit(cholesky)/cholesky | solution.py:19
  366.8 12.1 %cholesky.393 = f32[128,128]{1,0:T(8,128)S(1)} custom-call(f32[128,128]{1,0:T(8,128)S(1)} %cholesky.590), custom_call_target="Cholesky" | custom-call | tf_op jit(solution)/shard_map/jit(cholesky)/cholesky | solution.py:19
  378.9 9.8 %custom-call.32 = f32[1,128,128]{1,2,0:T(8,128)S(1)} custom-call(f32[1,128,128]{2,1,0:T(8,128)S(1)} %get-tuple-element.112), custom_call_target="InvertDiagBlocksLowerTriangular" | custom-call | tf_op jit(solution)/shard_map/jit(cholesky)/cholesky | solution.py:19
  390.3 11.7 %cholesky.414 = f32[128,128]{1,0:T(8,128)S(1)} custom-call(f32[128,128]{1,0:T(8,128)S(1)} %cholesky.595), custom_call_target="Cholesky" | custom-call | tf_op jit(solution)/shard_map/jit(cholesky)/cholesky | solution.py:19
  402.7 9.8 %custom-call.33 = f32[1,128,128]{1,2,0:T(8,128)S(1)} custom-call(f32[1,128,128]{2,1,0:T(8,128)S(1)} %get-tuple-element.109), custom_call_target="InvertDiagBlocksLowerTriangular" | custom-call | tf_op jit(solution)/shard_map/jit(cholesky)/cholesky | solution.py:19
  414.0 11.9 %cholesky.431 = f32[128,128]{1,0:T(8,128)S(1)} custom-call(f32[128,128]{1,0:T(8,128)S(1)} %convolution_subtract_fusion.14), custom_call_target="Cholesky" | custom-call | tf_op jit(solution)/shard_map/jit(cholesky)/cholesky | solution.py:19
  430.8 11.5 %while.8 = (s32[]{:T(128)}, f32[512,512]{1,0:T(8,128)}, s32[4,2]{0,1:T(2,128)S(1)}, f32[4,128,128]{2,1,0:T(8,128)S(1)}, s32[]{:T(128)}) while((s32[]{:T(128)}, f32[512,512]{1,0:T(8,128)}, s32[4,2]{0,1:T(2,128)S(1)}, f32[4,128,128]{2,1,0:T(8,128)S(1)}, s32[]{:T(128)}) %tuple.82), condition=%wide.while_cond.2, body=%wide.while_body.2.sunk | while | flops 2 | bytes 131181 | solution.py:20
  431.4 2.2 bitcast_dynamic-update-slice_fusion.6
  434.3 2.2 bitcast_dynamic-update-slice_fusion.6
  437.2 2.2 bitcast_dynamic-update-slice_fusion.6
  440.1 2.2 bitcast_dynamic-update-slice_fusion.6
  442.3 39.3 %custom-call.34 = f32[4,128,128]{1,2,0:T(8,128)S(1)} custom-call(f32[4,128,128]{2,1,0:T(8,128)S(1)} %get-tuple-element.51), custom_call_target="InvertDiagBlocksLowerTriangular" | custom-call | tf_op jit(solution)/shard_map/triangular_solve/custom-call.3 | solution.py:20
  483.4 2.1 convolution_subtract_fusion.5
  486.2 2.8 convolution_subtract_fusion.2
  489.6 4.0 fusion.40
  494.2 7.2 fusion
  502.7 3.7 fusion.162
  510.1 11.7 %cholesky.446 = f32[128,128]{1,0:T(8,128)S(1)} custom-call(f32[128,128]{1,0:T(8,128)S(1)} %cholesky.599), custom_call_target="Cholesky" | custom-call | tf_op jit(solution)/shard_map/jit(cholesky)/cholesky | solution.py:19
  522.0 9.9 %custom-call.35 = f32[1,128,128]{1,2,0:T(8,128)S(1)} custom-call(f32[1,128,128]{2,1,0:T(8,128)S(1)} %get-tuple-element.105), custom_call_target="InvertDiagBlocksLowerTriangular" | custom-call | tf_op jit(solution)/shard_map/jit(cholesky)/cholesky | solution.py:19
  534.5 11.7 %cholesky.465 = f32[128,128]{1,0:T(8,128)S(1)} custom-call(f32[128,128]{1,0:T(8,128)S(1)} %cholesky.603), custom_call_target="Cholesky" | custom-call | tf_op jit(solution)/shard_map/jit(cholesky)/cholesky | solution.py:19
  547.6 9.8 %custom-call.36 = f32[1,128,128]{1,2,0:T(8,128)S(1)} custom-call(f32[1,128,128]{2,1,0:T(8,128)S(1)} %get-tuple-element.102), custom_call_target="InvertDiagBlocksLowerTriangular" | custom-call | tf_op jit(solution)/shard_map/jit(cholesky)/cholesky | solution.py:19
  559.0 11.7 %cholesky.486 = f32[128,128]{1,0:T(8,128)S(1)} custom-call(f32[128,128]{1,0:T(8,128)S(1)} %cholesky.608), custom_call_target="Cholesky" | custom-call | tf_op jit(solution)/shard_map/jit(cholesky)/cholesky | solution.py:19
  571.4 10.0 %custom-call.37 = f32[1,128,128]{1,2,0:T(8,128)S(1)} custom-call(f32[1,128,128]{2,1,0:T(8,128)S(1)} %get-tuple-element.99), custom_call_target="InvertDiagBlocksLowerTriangular" | custom-call | tf_op jit(solution)/shard_map/jit(cholesky)/cholesky | solution.py:19
  582.9 11.7 %cholesky.503 = f32[128,128]{1,0:T(8,128)S(1)} custom-call(f32[128,128]{1,0:T(8,128)S(1)} %convolution_subtract_fusion.13), custom_call_target="Cholesky" | custom-call | tf_op jit(solution)/shard_map/jit(cholesky)/cholesky | solution.py:19
  598.9 11.8 %while.9 = (s32[]{:T(128)}, f32[512,512]{1,0:T(8,128)}, s32[4,2]{0,1:T(2,128)S(1)}, f32[4,128,128]{2,1,0:T(8,128)S(1)}, s32[]{:T(128)}) while((s32[]{:T(128)}, f32[512,512]{1,0:T(8,128)}, s32[4,2]{0,1:T(2,128)S(1)}, f32[4,128,128]{2,1,0:T(8,128)S(1)}, s32[]{:T(128)}) %tuple.97), condition=%wide.while_cond.2.clone, body=%wide.while_body.2.clone.sunk | while | flops 2 | bytes 131181 | solution.py:20
  599.6 2.3 bitcast_dynamic-update-slice_fusion.7
  602.6 2.3 bitcast_dynamic-update-slice_fusion.7
  605.5 2.3 bitcast_dynamic-update-slice_fusion.7
  608.5 2.2 bitcast_dynamic-update-slice_fusion.7
  610.7 39.7 %custom-call.38 = f32[4,128,128]{1,2,0:T(8,128)S(1)} custom-call(f32[4,128,128]{2,1,0:T(8,128)S(1)} %get-tuple-element.52), custom_call_target="InvertDiagBlocksLowerTriangular" | custom-call | tf_op jit(solution)/shard_map/triangular_solve/custom-call.3 | solution.py:20
  652.3 2.1 convolution_subtract_fusion.4
  655.0 2.8 convolution_subtract_fusion.1
  658.4 4.0 fusion.37
  663.0 6.9 fusion.8
  671.3 3.7 fusion.163
  678.7 11.7 %cholesky.518 = f32[128,128]{1,0:T(8,128)S(1)} custom-call(f32[128,128]{1,0:T(8,128)S(1)} %cholesky.612), custom_call_target="Cholesky" | custom-call | tf_op jit(solution)/shard_map/jit(cholesky)/cholesky | solution.py:19
  690.5 10.0 %custom-call.39 = f32[1,128,128]{1,2,0:T(8,128)S(1)} custom-call(f32[1,128,128]{2,1,0:T(8,128)S(1)} %get-tuple-element.95), custom_call_target="InvertDiagBlocksLowerTriangular" | custom-call | tf_op jit(solution)/shard_map/jit(cholesky)/cholesky | solution.py:19
  703.1 11.7 %cholesky.537 = f32[128,128]{1,0:T(8,128)S(1)} custom-call(f32[128,128]{1,0:T(8,128)S(1)} %cholesky.616), custom_call_target="Cholesky" | custom-call | tf_op jit(solution)/shard_map/jit(cholesky)/cholesky | solution.py:19
  716.1 9.8 %custom-call.40 = f32[1,128,128]{1,2,0:T(8,128)S(1)} custom-call(f32[1,128,128]{2,1,0:T(8,128)S(1)} %get-tuple-element.92), custom_call_target="InvertDiagBlocksLowerTriangular" | custom-call | tf_op jit(solution)/shard_map/jit(cholesky)/cholesky | solution.py:19
  727.5 11.7 %cholesky.558 = f32[128,128]{1,0:T(8,128)S(1)} custom-call(f32[128,128]{1,0:T(8,128)S(1)} %cholesky.621), custom_call_target="Cholesky" | custom-call | tf_op jit(solution)/shard_map/jit(cholesky)/cholesky | solution.py:19
  740.0 10.2 %custom-call.41 = f32[1,128,128]{1,2,0:T(8,128)S(1)} custom-call(f32[1,128,128]{2,1,0:T(8,128)S(1)} %get-tuple-element.89), custom_call_target="InvertDiagBlocksLowerTriangular" | custom-call | tf_op jit(solution)/shard_map/jit(cholesky)/cholesky | solution.py:19
  751.6 11.7 %cholesky.575 = f32[128,128]{1,0:T(8,128)S(1)} custom-call(f32[128,128]{1,0:T(8,128)S(1)} %convolution_subtract_fusion.12), custom_call_target="Cholesky" | custom-call | tf_op jit(solution)/shard_map/jit(cholesky)/cholesky | solution.py:19
  767.6 11.3 %while.10 = (s32[]{:T(128)}, f32[512,512]{1,0:T(8,128)}, s32[4,2]{0,1:T(2,128)S(1)}, f32[4,128,128]{2,1,0:T(8,128)S(1)}, s32[]{:T(128)}) while((s32[]{:T(128)}, f32[512,512]{1,0:T(8,128)}, s32[4,2]{0,1:T(2,128)S(1)}, f32[4,128,128]{2,1,0:T(8,128)S(1)}, s32[]{:T(128)}) %tuple.98), condition=%wide.while_cond.2.clone.1, body=%wide.while_body.2.clone.1.sunk | while | flops 2 | bytes 131181 | solution.py:20
  768.2 2.2 bitcast_dynamic-update-slice_fusion.8
  771.1 2.2 bitcast_dynamic-update-slice_fusion.8
  773.9 2.2 bitcast_dynamic-update-slice_fusion.8
  776.8 2.1 bitcast_dynamic-update-slice_fusion.8
  778.9 39.5 %custom-call.42 = f32[4,128,128]{1,2,0:T(8,128)S(1)} custom-call(f32[4,128,128]{2,1,0:T(8,128)S(1)} %get-tuple-element.53), custom_call_target="InvertDiagBlocksLowerTriangular" | custom-call | tf_op jit(solution)/shard_map/triangular_solve/custom-call.3 | solution.py:20
  820.3 2.1 convolution_subtract_fusion.3
  823.0 2.8 convolution_subtract_fusion
  826.4 4.0 fusion.34
  831.0 2.4 fusion.69
  (154 shorter events, 69.0 us)
Async XLA Ops:
  6.5 318.4 %copy-start = (f32[1024,512]{1,0:T(8,128)S(1)}, f32[1024,512]{1,0:T(8,128)}, u32[]{:S(2)}) copy-start(f32[1024,512]{1,0:T(8,128)} %param.18) | copy-start | bytes 6291460
  6.5 9.4 %copy-start.15 = (f32[2048]{0:T(1024)S(1)}, f32[2048]{0:T(1024)}, u32[]{:S(2)}) copy-start(f32[2048]{0:T(1024)} %param.14) | copy-start | bytes 24580
  6.5 76.7 %all-gather.3.cloned.1.call-start = ((), (), s32[]{:S(2)}) async-start(), calls=%async_computation | async-start | bytes 5242880 | tf_op jit(solution)/shard_map/all_gather | solution.py:59
  7.6 8.7 %collective-permute-start = (bf16[128,256]{1,0:T(8,128)(2,1)S(1)}, bf16[128,256]{1,0:T(8,128)(2,1)S(1)}, u32[]{:S(2)}, u32[]{:S(2)}) collective-permute-start(bf16[128,256]{1,0:T(8,128)(2,1)S(1)} %get-tuple-element.85), channel_id=1, source_target_pairs={{0,4},{4,8},{8,12},{12,16},{16,20},{20,24},{24,28},{28,32},{32,36}... | collective-permute-start | bytes 196616 | tf_op jit(solution)/shard_map/ppermute | solution.py:12
  12.5 9.2 %collective-permute-start.2 = (bf16[128,256]{1,0:T(8,128)(2,1)S(1)}, bf16[128,256]{1,0:T(8,128)(2,1)S(1)}, u32[]{:S(2)}, u32[]{:S(2)}) collective-permute-start(bf16[128,256]{1,0:T(8,128)(2,1)S(1)} %get-tuple-element.84), channel_id=1, source_target_pairs={{4,0},{8,4},{12,8},{16,12},{20,16},{24,20},{28,24},{32,28},{36,32}... | collective-permute-start | bytes 196616 | tf_op jit(solution)/shard_map/ppermute | solution.py:12
  16.0 4.0 copy-start.16
  16.0 7.7 copy-start.13
  16.0 11.3 %copy-start.14 = (f32[1,128,128]{2,1,0:T(8,128)S(1)}, f32[1,128,128]{2,1,0:T(8,128)}, u32[]{:S(2)}) copy-start(f32[1,128,128]{2,1,0:T(8,128)} %param.16) | copy-start | bytes 196612
  16.3 7.4 collective-permute-start.1
  21.7 5.6 collective-permute-start.3
  28.8 243.9 %all-reduce.3.cloned.1.call-start = ((), (), s32[]{:S(2)}) async-start(), calls=%async_computation.1 | async-start | bytes 2097152 | tf_op jit(solution)/shard_map/psum | solution.py:63
  88.1 236.9 %all-gather.5.cloned.1.call-start = ((), (), s32[]{:S(2)}) async-start(), calls=%async_computation.2 | async-start | bytes 5242880 | tf_op jit(solution)/shard_map/all_gather | solution.py:65
  333.8 1.4 copy-start.7
  341.6 1.0 copy-start.12
  481.6 4.6 copy-start.8
  488.9 5.2 copy-start.1
  501.3 1.4 copy-start.5
  509.2 1.0 copy-start.10
  650.4 4.6 copy-start.6
  657.8 5.2 copy-start.2
  669.9 1.3 copy-start.3
  677.7 1.0 copy-start.11
  818.4 4.6 copy-start.4
  825.8 5.3 copy-start.9
Sparse Core Ops, SparseCore 0:
  28.9 54.3 all-gather.2
  88.2 184.4 all-reduce.2
  275.0 49.8 all-gather.4
where the time goes:
time: 846 us; the launch traced here: 840 us
  other arithmetic  368 us (43%)
  waiting for transfers between devices  292 us (35%)
  matrix products  95.6 us (11%)
  local copies, waits for them, and re-layouts  48.9 us (6%)
  between operations  22.9 us (3%)
  starting transfers between devices  12.5 us (1%)
    another operation x44, other arithmetic, orthonormal(): lower = jnp.linalg.cholesky(correlation)  238 us
    psum x1, waiting for transfers between devices, shards(): gram_cols = lax.psum(gram_cols, 'rows') / total_rows  185 us
    another operation x7, other arithmetic, orthonormal(): lax.linalg.triangular_solve(lower, image, left_side=False, lower=True, tr...  122 us
    all_gather x1, waiting for transfers between devices, shards(): gathered = lax.all_gather(weighted, 'groups', axis=1, tiled=True)  54.4 us
    all_gather x1, waiting for transfers between devices, shards(): gram = lax.all_gather(gram_cols, 'groups', axis=1, tiled=True)  50 us
    another operation x21, matrix products, orthonormal(): lax.linalg.triangular_solve(lower, image, left_side=False, lower=True, tr...  37.5 us
    another operation x40, local copies, waits for them, and re-layouts, orthonormal(): lax.linalg.triangular_solve(lower, image, left_side=False, lower=True, tr...  34.4 us
    dot_general x3, matrix products, shards(): jnp.dot(gram, basis, precision=lax.Precision.HIGHEST, preferred_element_t...  22.9 us
  transfers between devices with their start and end apart: 7, of which 4 were waited for; matrix products, arithmetic and copies ran while one was open for 0% of the time, Pallas kernels for 0%

commit v1 on v0

v1 whole, which is shorter than its diff:
```python
import functools

import jax
import jax.numpy as jnp
from jax import lax
from jax.experimental import pallas as pl
from jax.experimental.pallas import tpu as pltpu
from jax.sharding import PartitionSpec as P

F32 = jnp.float32
BF16 = jnp.bfloat16
BLOCK = 128
PANEL = 8


def split(value):
    high = value.astype(BF16)
    return high, (value - high.astype(F32)).astype(BF16)


def dot3(left, right, dims):
    lh, ll = left
    rh, rl = right
    one = lambda a, b: lax.dot_general(a, b, (dims, ((), ())), preferred_element_type=F32)
    return one(lh, rh) + (one(lh, rl) + one(ll, rh))


def factor_block(m):
    n = m.shape[0]
    lanes = lax.broadcasted_iota(jnp.int32, (1, n), 1)
    subs = lax.broadcasted_iota(jnp.int32, (PANEL, n), 0)
    done = []
    for k in range(0, n, PANEL):
        top = m[:PANEL]
        rest = m[PANEL:]
        rows = [jnp.broadcast_to(top[a : a + 1], (PANEL, n)) for a in range(PANEL)]
        e = {}
        for a in range(PANEL):
            for j in range(a, PANEL):
                e[a, j] = jnp.broadcast_to(rows[a][:, k + j : k + j + 1], (PANEL, n))
        rows = [
            jnp.where(lanes == k + a, 1.0, jnp.where((lanes >= k) & (lanes < k + PANEL), 0.0, rows[a]))
            for a in range(PANEL)
        ]
        inv = []
        low = {}
        for a in range(PANEL):
            inv.append(1.0 / e[a, a])
            for b in range(a + 1, PANEL):
                low[b, a] = e[a, b] * inv[a]
            for b in range(a + 1, PANEL):
                for j in range(b, PANEL):
                    e[b, j] = e[b, j] - low[b, a] * e[a, j]
                rows[b] = rows[b] - low[b, a] * rows[a]
        out = rows[0] * lax.rsqrt(e[0, 0])
        for a in range(1, PANEL):
            out = jnp.where(subs == a, rows[a] * lax.rsqrt(e[a, a]), out)
        done.append(out)
        if k + PANEL == n:
            break
        q = [rows[a] * inv[a] for a in range(PANEL)]
        for a in reversed(range(PANEL)):
            for b in range(a + 1, PANEL):
                q[a] = q[a] - low[b, a] * q[b]
        height = n - k - PANEL
        inside = (lanes >= k) & (lanes < k + PANEL)
        acc = jnp.where(inside, 0.0, rest)
        for j in range(PANEL):
            col = jnp.broadcast_to(rest[:, k + j : k + j + 1], (height, n))
            acc = acc - col * q[j][:1]
        m = acc
    return jnp.concatenate(done, axis=0)


def inverse_factor(m_ref):
    n = m_ref.shape[0]
    cols = lax.broadcasted_iota(jnp.int32, (1, n), 1)
    rows = lax.broadcasted_iota(jnp.int32, (n, 1), 0)

    def step(j, carry):
        lo = pl.multiple_of(j * BLOCK, BLOCK)
        w = factor_block(m_ref[pl.ds(lo, BLOCK), pl.ds(lo, BLOCK)])
        r = lax.broadcasted_iota(jnp.int32, (BLOCK, BLOCK), 0)
        c = lax.broadcasted_iota(jnp.int32, (BLOCK, BLOCK), 1)
        w = jnp.where(r >= c, w, 0.0)
        ws = split(w)
        panel = m_ref[pl.ds(lo, BLOCK), :]
        z = dot3(ws, split(panel), ((1,), (0,)))
        m_ref[pl.ds(lo, BLOCK), :] = z
        m_ref[pl.ds(lo, BLOCK), pl.ds(lo, BLOCK)] = w
        z = m_ref[pl.ds(lo, BLOCK), :]
        y = jnp.where(cols >= lo + BLOCK, z, 0.0)
        below = rows >= lo + BLOCK
        inside = (cols >= lo) & (cols < lo + BLOCK)
        m = m_ref[...]
        m = jnp.where(below & inside, 0.0, m)
        m_ref[...] = m - dot3(split(y), split(z), ((0,), (0,)))
        return carry

    lax.fori_loop(0, n // BLOCK, step, 0)


def assemble(core, mine_ref, other_ref, gram_ref, gh_ref, gl_ref):
    n = gram_ref.shape[0]
    groups = 4
    size = n // groups
    lanes = size // 2

    def block(group, which, ref, half):
        lo = (group * 3 + which) * size
        return ref[lo : lo + size, :]

    at = pl.multiple_of(core * lanes, lanes)
    off = pl.multiple_of((1 - core) * lanes, lanes)
    for group in range(groups):
        col = group * size
        for which in range(3):
            row = ((group + which) % groups) * size
            for ref, shift in ((mine_ref, at), (other_ref, off)):
                gram_ref[row : row + size, pl.ds(pl.multiple_of(col + shift, lanes), lanes)] = block(group, which, ref, 0)
    for group in range(groups):
        a, b = group * size, ((group + 1) % groups) * size
        gram_ref[a : a + size, b : b + size] = gram_ref[b : b + size, a : a + size].T
    for group in range(groups // 2):
        a, b = group * size, (group + 2) * size
        both = gram_ref[b : b + size, a : a + size] + gram_ref[a : a + size, b : b + size].T
        gram_ref[b : b + size, a : a + size] = both
        gram_ref[a : a + size, b : b + size] = both.T
    gh, gl = split(gram_ref[...])
    gh_ref[...] = gh
    gl_ref[...] = gl


def iterate_kernel(iters, where_ref, mine_ref, other_ref, s_ref, out_ref, gram_ref, gh_ref, gl_ref, image_ref, basis_ref, m_ref):
    assemble(where_ref[1], mine_ref, other_ref, gram_ref, gh_ref, gl_ref)
    basis_ref[...] = s_ref[...]
    n = m_ref.shape[0]

    def turn_index(i, carry):
        bs = split(basis_ref[...])
        image_ref[...] = dot3((gh_ref[...], gl_ref[...]), bs, ((1,), (0,)))
        parts = split(image_ref[...])
        m_ref[...] = dot3(parts, parts, ((0,), (0,)))
        inverse_factor(m_ref)
        r = lax.broadcasted_iota(jnp.int32, (n, n), 0)
        c = lax.broadcasted_iota(jnp.int32, (n, n), 1)
        w = jnp.where(r >= c, m_ref[...], 0.0)
        basis_ref[...] = dot3(split(image_ref[...]), split(w), ((1,), (1,)))
        return carry

    lax.fori_loop(0, iters, turn_index, 0)
    groups = 4
    size = basis_ref.shape[0] // groups
    cols = n // groups
    group = where_ref[0]
    for q in range(groups):
        row = pl.multiple_of(lax.rem(group + q, groups) * size, size)
        part = basis_ref[pl.ds(row, size), pl.ds(pl.multiple_of(group * cols, cols), cols)]
        out_ref[q * size : (q + 1) * size, :] = part.astype(BF16)


def iterate(where, mine, other, start, iters):
    n, k = start.shape
    return pl.pallas_call(
        functools.partial(iterate_kernel, iters),
        out_shape=jax.ShapeDtypeStruct((n, k // 4), BF16),
        in_specs=[pl.BlockSpec(memory_space=pltpu.SMEM)] + [pl.BlockSpec(memory_space=pltpu.VMEM)] * 3,
        out_specs=pl.BlockSpec(memory_space=pltpu.VMEM),
        scratch_shapes=[
            pltpu.VMEM((n, n), F32),
            pltpu.VMEM((n, n), BF16),
            pltpu.VMEM((n, n), BF16),
            pltpu.VMEM((n, k), F32),
            pltpu.VMEM((n, k), F32),
            pltpu.VMEM((k, k), F32),
        ],
        compiler_params=pltpu.CompilerParams(vmem_limit_bytes=52 * 2**20),
        cost_estimate=pl.CostEstimate(flops=60 * 10**9, bytes_accessed=8 * 2**20, transcendentals=0),
    )(where, mine, other, start)


def modes_kernel(h, *refs):
    *pairs, basis_ref, out_ref = refs
    inner, rims = pairs[:4], pairs[4:]
    rows = out_ref.shape[0]
    size = basis_ref.shape[0] // 4

    def project(refs, lo, hi):
        total = None
        for q, ref in enumerate(refs):
            term = jnp.dot(ref[lo:hi, :], basis_ref[q * size : (q + 1) * size, :], preferred_element_type=F32)
            total = term if total is None else total + term
        return total

    out_ref[:h, :] = project(rims, 0, h)
    out_ref[rows - h :, :] = project(rims, h, 2 * h)
    out_ref[h : rows - h, :] = project(inner, 0, rows - 2 * h)


def modes(own, following, across, behind, basis, rows, h):
    parts = [[p[i] for p in (own, following, across, behind)] for i in (0, 1)]
    return pl.pallas_call(
        functools.partial(modes_kernel, h),
        out_shape=jax.ShapeDtypeStruct((rows, basis.shape[1]), F32),
        in_specs=[pl.BlockSpec(memory_space=pltpu.VMEM)] * 9,
        out_specs=pl.BlockSpec(memory_space=pltpu.VMEM),
        compiler_params=pltpu.CompilerParams(vmem_limit_bytes=40 * 2**20),
    )(*parts[0], *parts[1], basis)


ITERS = 3
ROWS = ("y", "z", "core")


def shift_rows(value, by):
    blocks = lax.axis_size("y") * lax.axis_size("z") * lax.axis_size("core")
    pairs = [(i, i + by) for i in range(blocks) if 0 <= i + by < blocks]
    return lax.ppermute(value, ROWS, pairs)


def turn(value, axis, by):
    size = lax.axis_size(axis)
    return lax.ppermute(value, axis, [(i, (i + by) % size) for i in range(size)])


def spread(value, axis):
    size = 1
    for name in axis if isinstance(axis, tuple) else (axis,):
        size *= lax.axis_size(name)
    copies = jnp.broadcast_to(value[None], (size,) + value.shape).reshape((size * value.shape[0],) + value.shape[1:])
    return lax.all_to_all(copies, axis, 0, 0, tiled=True)


def cross(left, right):
    return lax.dot_general(left, right, (((0,), (0,)), ((), ())), preferred_element_type=F32)


def rim(snaps, mass, coupling, near, far, offset):
    other = jnp.where(offset == 1, near, far).astype(F32)
    terms = jnp.dot(coupling, other, precision=lax.Precision.HIGHEST, preferred_element_type=F32)
    return (mass[:, None] * snaps.astype(F32) + terms).astype(BF16)


def shards(snapshots, mass_diag, lower_coupling, upper_coupling, band_offsets, start_basis):
    block_rows, width = snapshots.shape
    h = lower_coupling.shape[1]
    total_rows = block_rows * lax.axis_size(ROWS)
    group = lax.axis_index("x")
    core = lax.axis_index("core")

    top, bottom = snapshots[:h], snapshots[block_rows - h :]
    below = [shift_rows(bottom, 1), shift_rows(bottom, 2)]
    above = [shift_rows(top, -1), shift_rows(top, -2)]
    inner = (mass_diag[h : block_rows - h, None] * snapshots[h : block_rows - h].astype(F32)).astype(BF16)
    rims = jnp.concatenate(
        [
            rim(top, mass_diag[:h], lower_coupling[0], below[0], below[1], band_offsets[0, 0]),
            rim(bottom, mass_diag[block_rows - h :], upper_coupling[0], above[0], above[1], band_offsets[0, 1]),
        ],
        axis=0,
    )

    own, following, facing = [], [], []
    for piece in (inner, rims):
        part = piece.shape[0] // 2
        first = group < 2
        own_half = lax.dynamic_slice_in_dim(piece, jnp.where(first, 0, part), part, 0)
        send_half = lax.dynamic_slice_in_dim(piece, jnp.where(first, part, 0), part, 0)
        own.append(piece)
        following.append(turn(piece, "x", -1))
        facing.append((turn(send_half, "x", 2), own_half))
    blocks = [
        sum(cross(p, p) for p in own),
        sum(cross(f, p) for f, p in zip(following, own)),
        sum(cross(f, p) for f, p in facing),
    ]
    partial = jnp.concatenate(blocks, axis=0)
    lanes = width // 2
    keep = lax.dynamic_slice_in_dim(partial, core * lanes, lanes, 1)
    give = lax.dynamic_slice_in_dim(partial, (1 - core) * lanes, lanes, 1)
    chip = keep + turn(give, "core", 1)
    sources = lax.axis_size(("y", "z"))
    pieces = lax.all_to_all(chip, ("y", "z"), 0, 0, tiled=True)
    share = pieces.reshape((sources, -1, lanes)).sum(0) / total_rows
    halves = spread(spread(share, "z"), ("x", "y"))
    other_halves = turn(halves, "core", 1)

    own, following, halves, other_halves = lax.optimization_barrier((own, following, halves, other_halves))
    behind = [turn(p, "x", 1) for p in own]
    across = [turn(p, "x", 2) for p in own]
    where = jnp.stack([group, core]).astype(jnp.int32)
    basis = iterate(where, halves, other_halves, start_basis, ITERS)
    return modes(own, following, across, behind, basis, block_rows, h)


def solution(mesh):
    fine = jax.sharding.Mesh(mesh.devices.reshape(4, 8, 2, 4), ("y", "z", "core", "x"))
    placed = (
        P(ROWS, "x"),
        P(ROWS),
        P(ROWS, None, None),
        P(ROWS, None, None),
        P(ROWS, None),
        P(),
    )
    return jax.shard_map(shards, mesh=fine, in_specs=placed, out_specs=P(ROWS, "x"), check_vma=False)
```

time: 846 us -> 240 us (0.28)
  other arithmetic: 368 us -> 1.86 us
  waiting for transfers between devices: 292 us -> 28.2 us
  Pallas kernels: 0 us -> 110 us
  matrix products: 95.6 us -> 4.04 us
  blocking collectives: 0 us -> 63.6 us
  local copies, waits for them, and re-layouts: 48.9 us -> 3.9 us
  between operations: 22.9 us -> 1.49 us
  starting transfers between devices: 12.5 us -> 26.3 us
    another operation x51 -> x1, other arithmetic: 360 us -> 0.07 us  [shards(): where = jnp.stack([group, core]).astype(jnp.int32)]
    psum x1 -> x0, waiting for transfers between devices: 185 us -> none  [shards(): gram_cols = lax.psum(gram_cols, 'rows') / total_rows]
    pallas_call x0 -> x2, Pallas kernels: none -> 110 us  [the longest x1 108 us: iterate(): pl.pallas_call(functools.partial(iterate_kernel, iters), out_shape=jax.Sh...]
    all_gather x2 -> x0, waiting for transfers between devices: 104 us -> none  [the longest x1 54.4 us: shards(): gathered = lax.all_gather(weighted, 'groups', axis=1, tiled=True)]
    all_to_all x0 -> x3, blocking collectives: none -> 63.6 us  [the longest x2 38.6 us: spread(): return lax.all_to_all(copies, axis, 0, 0, tiled=True)]
    another operation x39 -> x0, matrix products: 54 us -> none  [the longest x21 37.5 us: orthonormal(): lax.linalg.triangular_solve(lower, image, left_side=False, lower=True, tr...]
    dot_general x10 -> x8, matrix products: 41.7 us -> 4.04 us  [the longest x2 2.1 us: rim(): jnp.dot(coupling, other, precision=lax.Precision.HIGHEST, preferred_eleme...]
    another operation x52 -> x0, local copies, waits for them, and re-layouts: 34.8 us -> none  [the longest x40 34.4 us: orthonormal(): lax.linalg.triangular_solve(lower, image, left_side=False, lower=True, tr...]
  transfers between devices with their start and end apart: 7 -> 14, of which waited for: 4 -> 4; matrix products, arithmetic and copies ran while one was open for 0% -> 3% of each run, Pallas kernels for 0% -> 45%
where the time goes in v1:
time: 240 us; the launch traced here: 239 us
  Pallas kernels  110 us (46%)
  blocking collectives  63.6 us (26%)
  waiting for transfers between devices  28.2 us (12%)
  starting transfers between devices  26.3 us (11%)
  matrix products  4.04 us (2%)
  local copies, waits for them, and re-layouts  3.9 us (2%)
    pallas_call x1, Pallas kernels, iterate(): pl.pallas_call(functools.partial(iterate_kernel, iters), out_shape=jax.Sh...  108 us
    all_to_all x2, blocking collectives, spread(): return lax.all_to_all(copies, axis, 0, 0, tiled=True)  38.6 us
    ppermute x10, waiting for transfers between devices, turn(): lax.ppermute(value, axis, [(i, (i + by) % size) for i in range(size)])  28.2 us
    all_to_all x1, blocking collectives, shards(): pieces = lax.all_to_all(chip, ('y', 'z'), 0, 0, tiled=True)  25 us
    ppermute x10, starting transfers between devices, turn(): lax.ppermute(value, axis, [(i, (i + by) % size) for i in range(size)])  14.6 us
    ppermute x4, starting transfers between devices, shift_rows(): return lax.ppermute(value, ROWS, pairs)  11.7 us
  transfers between devices with their start and end apart: 14, of which 4 were waited for; matrix products, arithmetic and copies ran while one was open for 3% of the time, Pallas kernels for 45%

profile of v1, /device:TPU:1, one launch (start us, length us, event | category | flops | bytes accessed | tf_op | source)
XLA Modules:
  0.0 239.1 jit_solution(13687835303520944276)
XLA Ops:
  0.0 0.0 copy-start
  0.0 0.9 fusion.19
  0.9 4.9 %collective-permute-start = (bf16[128,256]{1,0:T(8,128)(2,1)S(1)}, bf16[128,256]{1,0:T(8,128)(2,1)S(1)}, u32[]{:S(2)}, u32[]{:S(2)}) collective-permute-start(bf16[128,256]{1,0:T(8,128)(2,1)S(1)} %get-tuple-element.17), channel_id=1, source_target_pairs={{0,4},{4,8},{8,12},{12,16},{16,20},{20,24},{24,28},{28,32},{32,36}... | collective-permute-start | bytes 196616 | tf_op jit(solution)/shard_map/ppermute | solution.py:218
  5.9 3.5 %collective-permute-start.1 = (bf16[128,256]{1,0:T(8,128)(2,1)S(1)}, bf16[128,256]{1,0:T(8,128)(2,1)S(1)}, u32[]{:S(2)}, u32[]{:S(2)}) collective-permute-start(bf16[128,256]{1,0:T(8,128)(2,1)S(1)} %get-tuple-element.17), channel_id=1, source_target_pairs={{0,8},{4,12},{8,16},{12,20},{16,24},{20,28},{24,32},{28,36},{32,40... | collective-permute-start | bytes 196616 | tf_op jit(solution)/shard_map/ppermute | solution.py:218
  9.4 1.9 collective-permute-start.2
  11.3 1.3 collective-permute-start.3
  12.6 0.7 slice.24
  13.3 0.0 copy-start.2
  13.3 1.5 multiply_convert_fusion.refs_0_
  14.8 0.0 copy-start.1
  14.9 2.6 %collective-permute-start.4 = (bf16[1792,256]{1,0:T(8,128)(2,1)S(1)}, bf16[1792,256]{1,0:T(8,128)(2,1)S(1)}, u32[]{:S(2)}, u32[]{:S(2)}) collective-permute-start(bf16[1792,256]{1,0:T(8,128)(2,1)S(1)} %multiply_convert_fusion.refs_0_), channel_id=1, source_target_pairs={{0,3},{1,0},{2,1},{3,2},{4,7},{5,4},{6,5},{7,6},{8,11},{9,8},{10,9... | collective-permute-start | bytes 2752520 | tf_op jit(solution)/shard_map/ppermute | solution.py:223
  17.4 0.7 fusion.20
  18.1 0.4 fusion.22
  18.6 0.0 copy-done.2
  18.6 0.6 fusion.21
  20.4 0.0 collective-permute-done
  20.4 0.6 collective-permute-start.6
  21.0 0.0 collective-permute-done.1
  21.1 0.0 copy-done
  21.1 1.0 fusion.2
  22.1 0.0 collective-permute-done.2
  22.1 0.0 collective-permute-done.3
  22.1 0.0 copy-done.1
  22.1 1.0 fusion.3
  23.2 0.1 fusion.5
  23.4 2.5 %collective-permute-start.7 = (bf16[128,256]{1,0:T(8,128)(2,1)S(1)}, bf16[128,256]{1,0:T(8,128)(2,1)S(1)}, u32[]{:S(2)}, u32[]{:S(2)}) collective-permute-start(bf16[128,256]{1,0:T(8,128)(2,1)S(1)} %fusion.5), channel_id=1, source_target_pairs={{0,2},{1,3},{2,0},{3,1},{4,6},{5,7},{6,4},{7,5},{8,10},{9,11},{10,... | collective-permute-start | bytes 196616 | tf_op jit(solution)/shard_map/ppermute | solution.py:223
  25.9 0.6 collective-permute-start.5
  26.4 0.2 convolution_add_fusion.1
  26.7 7.9 %collective-permute-done.7 = bf16[128,256]{1,0:T(8,128)(2,1)S(1)} collective-permute-done((bf16[128,256]{1,0:T(8,128)(2,1)S(1)}, bf16[128,256]{1,0:T(8,128)(2,1)S(1)}, u32[]{:S(2)}, u32[]{:S(2)}) %collective-permute-start.7) | collective-permute-done | bytes 65568 | tf_op jit(solution)/shard_map/ppermute | solution.py:223
  34.6 0.3 fusion.7
  34.8 15.4 %collective-permute-done.5.refs_5_ = bf16[256,256]{1,0:T(8,128)(2,1)S(1)} collective-permute-done((bf16[256,256]{1,0:T(8,128)(2,1)S(1)}, bf16[256,256]{1,0:T(8,128)(2,1)S(1)}, u32[]{:S(2)}, u32[]{:S(2)}) %collective-permute-start.5) | collective-permute-done | bytes 131104 | tf_op jit(solution)/shard_map/ppermute | solution.py:223
  50.2 0.2 fusion.18
  50.5 0.0 collective-permute-done.6
  50.5 0.4 convolution_add_fusion.2
  50.8 0.0 collective-permute-done.4.refs_1_
  50.8 0.4 convolution_add_fusion
  51.3 0.1 pad_maximum_fusion
  51.4 0.8 constant_dynamic-slice_fusion
  52.1 0.0 collective-permute-start.8
  52.1 1.9 collective-permute-done.8
  54.1 0.1 dynamic-slice_add_fusion
  54.1 25.0 %all_to_all.24 = f32[32,24,128]{2,1,0:T(8,128)S(1)} all-to-all(f32[32,24,128]{2,1,0:T(8,128)S(1)} %bitcast.34), channel_id=1, replica_groups=mesh['y'=4,'z'=8,'core'=2,'x'=4] {'y','z'}, dimensions={0} | all-to-all | bytes 786432 | tf_op jit(solution)/shard_map/all_to_all | solution.py:283
  79.2 13.0 %all_to_all.25 = f32[8,24,128]{2,1,0:T(8,128)S(1)} all-to-all(f32[8,24,128]{2,1,0:T(8,128)S(1)} %broadcast_in_dim.6), channel_id=1, replica_groups=mesh['y'=4,'z'=8,'core'=2,'x'=4] {'z'}, dimensions={0} | all-to-all | bytes 196608 | tf_op jit(solution)/shard_map/all_to_all | solution.py:231
  92.2 0.1 broadcast_in_dim.8
  92.3 25.6 %all_to_all.26 = f32[16,192,128]{2,1,0:T(8,128)S(1)} all-to-all(f32[16,192,128]{2,1,0:T(8,128)S(1)} %broadcast_in_dim.8), channel_id=1, replica_groups=mesh['y'=4,'z'=8,'core'=2,'x'=4] {'x','y'}, dimensions={0} | all-to-all | bytes 3145728 | tf_op jit(solution)/shard_map/all_to_all | solution.py:231
  117.9 4.2 %collective-permute-start.9 = (f32[3072,128]{1,0:T(8,128)S(1)}, f32[3072,128]{1,0:T(8,128)S(1)}, u32[]{:S(2)}, u32[]{:S(2)}) collective-permute-start(f32[3072,128]{1,0:T(8,128)S(1)} %bitcast.32), channel_id=1, source_target_pairs={{0,4},{4,0},{1,5},{5,1},{2,6},{6,2},{3,7},{7,3},{8,12},{12,8},{9,1... | collective-permute-start | bytes 4718600 | tf_op jit(solution)/shard_map/ppermute | solution.py:223
  122.2 0.1 pad_add_fusion.where_ref
  122.2 3.0 %collective-permute-done.9.other_ref = f32[3072,128]{1,0:T(8,128)S(1)} collective-permute-done((f32[3072,128]{1,0:T(8,128)S(1)}, f32[3072,128]{1,0:T(8,128)S(1)}, u32[]{:S(2)}, u32[]{:S(2)}) %collective-permute-start.9) | collective-permute-done | bytes 1572896 | tf_op jit(solution)/shard_map/ppermute | solution.py:223
  125.2 0.0 copy-start.3
  125.2 0.8 collective-permute-start.10
  126.0 0.6 collective-permute-start.11
  126.6 1.6 collective-permute-start.12
  128.2 1.1 collective-permute-start.13
  129.3 0.0 copy-done.3
  129.3 107.5 %shard_map.64.refs_8_ = bf16[1024,128]{1,0:T(8,128)(2,1)S(1)} custom-call(s32[2]{0:T(128)S(1)} %pad_add_fusion.where_ref, f32[3072,128]{1,0:T(8,128)S(1)} %bitcast.33, f32[3072,128]{1,0:T(8,128)} %copy-done.3, f32[1024,512]{1,0:T(8,128)} %s_ref.1), custom_call_target="tpu_custom_call" | custom-call | flops 60000002048 | bytes 8388608 | tf_op jit(solution)/shard_map/pallas_call | solution.py:164
  236.8 0.0 collective-permute-done.12.refs_6_
  236.9 0.0 collective-permute-done.13.refs_7_
  236.9 0.0 collective-permute-done.10.refs_2_
  236.9 0.0 collective-permute-done.11.refs_3_
  236.9 2.2 shard_map.65
  (5 shorter events, 0.1 us)
Async XLA Ops:
  0.0 21.1 %copy-start = (f32[1,128,128]{2,1,0:T(8,128)S(1)}, f32[1,128,128]{2,1,0:T(8,128)}, u32[]{:S(2)}) copy-start(f32[1,128,128]{2,1,0:T(8,128)} %param.8) | copy-start | bytes 196612
  0.9 19.5 %collective-permute-start = (bf16[128,256]{1,0:T(8,128)(2,1)S(1)}, bf16[128,256]{1,0:T(8,128)(2,1)S(1)}, u32[]{:S(2)}, u32[]{:S(2)}) collective-permute-start(bf16[128,256]{1,0:T(8,128)(2,1)S(1)} %get-tuple-element.17), channel_id=1, source_target_pairs={{0,4},{4,8},{8,12},{12,16},{16,20},{20,24},{24,28},{28,32},{32,36}... | collective-permute-start | bytes 196616 | tf_op jit(solution)/shard_map/ppermute | solution.py:218
  5.9 15.2 %collective-permute-start.1 = (bf16[128,256]{1,0:T(8,128)(2,1)S(1)}, bf16[128,256]{1,0:T(8,128)(2,1)S(1)}, u32[]{:S(2)}, u32[]{:S(2)}) collective-permute-start(bf16[128,256]{1,0:T(8,128)(2,1)S(1)} %get-tuple-element.17), channel_id=1, source_target_pairs={{0,8},{4,12},{8,16},{12,20},{16,24},{20,28},{24,32},{28,36},{32,40... | collective-permute-start | bytes 196616 | tf_op jit(solution)/shard_map/ppermute | solution.py:218
  9.4 12.7 %collective-permute-start.2 = (bf16[128,256]{1,0:T(8,128)(2,1)S(1)}, bf16[128,256]{1,0:T(8,128)(2,1)S(1)}, u32[]{:S(2)}, u32[]{:S(2)}) collective-permute-start(bf16[128,256]{1,0:T(8,128)(2,1)S(1)} %get-tuple-element.18), channel_id=1, source_target_pairs={{4,0},{8,4},{12,8},{16,12},{20,16},{24,20},{28,24},{32,28},{36,32}... | collective-permute-start | bytes 196616 | tf_op jit(solution)/shard_map/ppermute | solution.py:218
  11.3 10.8 %collective-permute-start.3 = (bf16[128,256]{1,0:T(8,128)(2,1)S(1)}, bf16[128,256]{1,0:T(8,128)(2,1)S(1)}, u32[]{:S(2)}, u32[]{:S(2)}) collective-permute-start(bf16[128,256]{1,0:T(8,128)(2,1)S(1)} %get-tuple-element.18), channel_id=1, source_target_pairs={{8,0},{12,4},{16,8},{20,12},{24,16},{28,20},{32,24},{36,28},{40,32... | collective-permute-start | bytes 196616 | tf_op jit(solution)/shard_map/ppermute | solution.py:218
  13.3 5.2 %copy-start.2 = (s32[1,2]{1,0:T(1,128)S(1)}, s32[1,2]{1,0:T(1,128)}, u32[]{:S(2)}) copy-start(s32[1,2]{1,0:T(1,128)} %param.10) | copy-start | bytes 28
  14.8 7.3 %copy-start.1 = (f32[1,128,128]{2,1,0:T(8,128)S(1)}, f32[1,128,128]{2,1,0:T(8,128)}, u32[]{:S(2)}) copy-start(f32[1,128,128]{2,1,0:T(8,128)} %param.9) | copy-start | bytes 196612
  14.9 36.0 %collective-permute-start.4 = (bf16[1792,256]{1,0:T(8,128)(2,1)S(1)}, bf16[1792,256]{1,0:T(8,128)(2,1)S(1)}, u32[]{:S(2)}, u32[]{:S(2)}) collective-permute-start(bf16[1792,256]{1,0:T(8,128)(2,1)S(1)} %multiply_convert_fusion.refs_0_), channel_id=1, source_target_pairs={{0,3},{1,0},{2,1},{3,2},{4,7},{5,4},{6,5},{7,6},{8,11},{9,8},{10,9... | collective-permute-start | bytes 2752520 | tf_op jit(solution)/shard_map/ppermute | solution.py:223
  20.4 30.0 %collective-permute-start.6 = (bf16[896,256]{1,0:T(8,128)(2,1)S(1)}, bf16[896,256]{1,0:T(8,128)(2,1)S(1)}, u32[]{:S(2)}, u32[]{:S(2)}) collective-permute-start(bf16[896,256]{1,0:T(8,128)(2,1)S(1)} %constant_dynamic-slice_fusion.1), channel_id=1, source_target_pairs={{0,2},{1,3},{2,0},{3,1},{4,6},{5,7},{6,4},{7,5},{8,10},{9,11},{10,... | collective-permute-start | bytes 1376264 | tf_op jit(solution)/shard_map/ppermute | solution.py:223
  23.4 11.2 %collective-permute-start.7 = (bf16[128,256]{1,0:T(8,128)(2,1)S(1)}, bf16[128,256]{1,0:T(8,128)(2,1)S(1)}, u32[]{:S(2)}, u32[]{:S(2)}) collective-permute-start(bf16[128,256]{1,0:T(8,128)(2,1)S(1)} %fusion.5), channel_id=1, source_target_pairs={{0,2},{1,3},{2,0},{3,1},{4,6},{5,7},{6,4},{7,5},{8,10},{9,11},{10,... | collective-permute-start | bytes 196616 | tf_op jit(solution)/shard_map/ppermute | solution.py:223
  25.9 24.3 %collective-permute-start.5 = (bf16[256,256]{1,0:T(8,128)(2,1)S(1)}, bf16[256,256]{1,0:T(8,128)(2,1)S(1)}, u32[]{:S(2)}, u32[]{:S(2)}) collective-permute-start(bf16[256,256]{1,0:T(8,128)(2,1)S(1)} %pad_maximum_fusion.1.refs_4_), channel_id=1, source_target_pairs={{0,3},{1,0},{2,1},{3,2},{4,7},{5,4},{6,5},{7,6},{8,11},{9,8},{10,9... | collective-permute-start | bytes 393224 | tf_op jit(solution)/shard_map/ppermute | solution.py:223
  52.1 1.9 collective-permute-start.8
  117.9 7.3 %collective-permute-start.9 = (f32[3072,128]{1,0:T(8,128)S(1)}, f32[3072,128]{1,0:T(8,128)S(1)}, u32[]{:S(2)}, u32[]{:S(2)}) collective-permute-start(f32[3072,128]{1,0:T(8,128)S(1)} %bitcast.32), channel_id=1, source_target_pairs={{0,4},{4,0},{1,5},{5,1},{2,6},{6,2},{3,7},{7,3},{8,12},{12,8},{9,1... | collective-permute-start | bytes 4718600 | tf_op jit(solution)/shard_map/ppermute | solution.py:223
  125.2 4.1 %copy-start.3 = (f32[3072,128]{1,0:T(8,128)}, f32[3072,128]{1,0:T(8,128)S(1)}, u32[]{:S(2)}) copy-start(f32[3072,128]{1,0:T(8,128)S(1)} %collective-permute-done.9.other_ref) | copy-start | bytes 4718596
  125.2 111.7 %collective-permute-start.10 = (bf16[1792,256]{1,0:T(8,128)(2,1)S(1)}, bf16[1792,256]{1,0:T(8,128)(2,1)S(1)}, u32[]{:S(2)}, u32[]{:S(2)}) collective-permute-start(bf16[1792,256]{1,0:T(8,128)(2,1)S(1)} %multiply_convert_fusion.refs_0_), channel_id=1, source_target_pairs={{0,2},{1,3},{2,0},{3,1},{4,6},{5,7},{6,4},{7,5},{8,10},{9,11},{10,... | collective-permute-start | bytes 2752520 | tf_op jit(solution)/shard_map/ppermute | solution.py:223
  126.0 110.8 %collective-permute-start.11 = (bf16[1792,256]{1,0:T(8,128)(2,1)S(1)}, bf16[1792,256]{1,0:T(8,128)(2,1)S(1)}, u32[]{:S(2)}, u32[]{:S(2)}) collective-permute-start(bf16[1792,256]{1,0:T(8,128)(2,1)S(1)} %multiply_convert_fusion.refs_0_), channel_id=1, source_target_pairs={{0,1},{1,2},{2,3},{3,0},{4,5},{5,6},{6,7},{7,4},{8,9},{9,10},{10,1... | collective-permute-start | bytes 2752520 | tf_op jit(solution)/shard_map/ppermute | solution.py:223
  126.6 110.2 %collective-permute-start.12 = (bf16[256,256]{1,0:T(8,128)(2,1)S(1)}, bf16[256,256]{1,0:T(8,128)(2,1)S(1)}, u32[]{:S(2)}, u32[]{:S(2)}) collective-permute-start(bf16[256,256]{1,0:T(8,128)(2,1)S(1)} %pad_maximum_fusion.1.refs_4_), channel_id=1, source_target_pairs={{0,2},{1,3},{2,0},{3,1},{4,6},{5,7},{6,4},{7,5},{8,10},{9,11},{10,... | collective-permute-start | bytes 393224 | tf_op jit(solution)/shard_map/ppermute | solution.py:223
  128.2 108.6 %collective-permute-start.13 = (bf16[256,256]{1,0:T(8,128)(2,1)S(1)}, bf16[256,256]{1,0:T(8,128)(2,1)S(1)}, u32[]{:S(2)}, u32[]{:S(2)}) collective-permute-start(bf16[256,256]{1,0:T(8,128)(2,1)S(1)} %pad_maximum_fusion.1.refs_4_), channel_id=1, source_target_pairs={{0,1},{1,2},{2,3},{3,0},{4,5},{5,6},{6,7},{7,4},{8,9},{9,10},{10,1... | collective-permute-start | bytes 393224 | tf_op jit(solution)/shard_map/ppermute | solution.py:223
